TPU v7x, 128 devices: a whole 4x4x4 slice. The times are simulated.
128 devices in a mesh: tm: 32 (over y, x_lo, z), row: 4 (over x_hi, core).
Axes of the slice: x: 4 (x_hi: 2, x_lo: 2; x = x_hi * 2 + x_lo), y: 4, z: 4, core: 2. Of those that a mesh axis runs over, the one named last changes fastest.
Arguments:
- latents: bfloat16 [256, 8, 32, 320], P('tm', 'row'), may hold values from -6 to 6
- window_shift: int32 [1], replicated, may hold values from 1 to 7
- timesteps: int32 [32], P('tm'), may hold values from 0 to 999
- motion_gain: float32 [320], replicated, may hold values from 0.25 to 1.75
- time_weight: float32 [320, 320], replicated, may hold values from -0.3125 to 0.3125
- qkv_weight: bfloat16 [320, 960], replicated, may hold values from -0.3125 to 0.3125
- attn_out_weight: bfloat16 [320, 320], replicated, may hold values from -0.3125 to 0.3125
- spatial_gain: float32 [320], replicated, may hold values from 0.25 to 1.75
- conv_weight: bfloat16 [9, 320, 1280], replicated, may hold values from -0.109375 to 0.109375
- proj_weight: bfloat16 [1280, 320], replicated, may hold values from -0.15625 to 0.15625
- out_cotangent: bfloat16 [256, 8, 32, 320], P('tm', 'row'), may hold values from -6 to 6
Outputs:
- block_output: bfloat16 [256, 8, 32, 320], P('tm', 'row')
- grad_input: float32 [256, 8, 32, 320], P('tm', 'row')
- grad_weights: float32 [512000], P(('tm', 'row'))
All inputs are finite; a program needn't handle non-finite values.
Results may differ from a plain program's by a relative error of at most 0.017.
Values may be sent and summed in bfloat16 or wider, within the bound.
A program may use at most 128 MiB of HBM per device.

v0:
```python
import math

import jax
import jax.numpy as jnp
from jax import lax
from jax.experimental import pallas as pl
from jax.experimental.pallas import tpu as pltpu
from jax.sharding import PartitionSpec as P

BF = jnp.bfloat16
F32 = jnp.float32
MESH = pl.DeviceIdType.MESH
VMEM = pltpu.VMEM

FR = 8
CELLS = 64
COLS = 32
CH = 320
HID = 1280
HEADS = 8
HD = 40
HP = 64
BLOCKS = 4
BC = CELLS // BLOCKS
PADQ = HEADS * HP
PADZ = 3 * PADQ
SCALE = 1.0 / math.sqrt(HD)
EXP2 = SCALE * math.log2(math.e)
EPS = 1e-06
VLIM = 56 * 1024 * 1024


def mm(a, b):
    return jnp.dot(a, b, preferred_element_type=F32)


def mm_nt(a, b):
    return lax.dot_general(a, b, (((1,), (1,)), ((), ())), preferred_element_type=F32)


def mm_tn(a, b):
    return lax.dot_general(a, b, (((0,), (0,)), ((), ())), preferred_element_type=F32)


def rms_scale(values):
    return lax.rsqrt(jnp.mean(values * values, axis=-1, keepdims=True) + EPS)


def rms_back(values, gain, cotangent):
    r = rms_scale(values)
    g = cotangent * gain
    return r * g - values * (r * r * r) * jnp.mean(g * values, axis=-1, keepdims=True)


def parts_of(row):
    first = row.astype(BF).astype(F32)
    rest = row - first
    second = rest.astype(BF).astype(F32)
    return first, second, rest - second


def stack_parts(row):
    a, b, c = parts_of(row)
    at = lax.broadcasted_iota(jnp.int32, (16, row.shape[1]), 0)
    return jnp.where(at == 0, a, jnp.where(at == 1, b, jnp.where(at == 2, c, 0.0))).astype(BF)


def outer(left, right):
    a, b, _ = parts_of(left)
    c, d, _ = parts_of(right)
    at = lax.broadcasted_iota(jnp.int32, (16, left.shape[1]), 0)
    lhs = jnp.where(at < 4, jnp.where(at % 2 == 0, a, b), 0.0).astype(BF)
    at = lax.broadcasted_iota(jnp.int32, (16, right.shape[1]), 0)
    rhs = jnp.where(at < 4, jnp.where(at < 2, c, d), 0.0).astype(BF)
    return mm_tn(lhs, rhs)


def greet(peers):
    barrier = pltpu.get_barrier_semaphore()
    for peer in peers:
        pl.semaphore_signal(barrier, inc=1, device_id=peer, device_id_type=MESH)
    pl.semaphore_wait(barrier, len(peers))


def remote(src, dst, send, recv, peer):
    return pltpu.make_async_remote_copy(
        src_ref=src, dst_ref=dst, send_sem=send, recv_sem=recv, device_id=peer, device_id_type=MESH
    )


def ring():
    at, count = lax.axis_index("tm"), lax.axis_size("tm")
    row = lax.axis_index("row")
    return ((at + count - 1) % count, row), ((at + 1) % count, row)


def pair_masks():
    lane = lax.broadcasted_iota(jnp.int32, (128, 128), 1)
    return lane < HP


def both_heads(x, first):
    zero = jnp.zeros_like(x)
    return jnp.concatenate([jnp.where(first, x, zero), jnp.where(first, zero, x)], axis=0)


def pair_probs(q, kst, same):
    s = mm_nt(q, kst)
    e = jnp.where(same, jnp.exp2(s * EXP2), 0.0)
    ea, eb = e[:, :128], e[:, 128:]
    return jnp.concatenate(
        [
            ea * (1.0 / jnp.sum(ea, axis=-1, keepdims=True)),
            eb * (1.0 / jnp.sum(eb, axis=-1, keepdims=True)),
        ],
        axis=1,
    )


def same_cell():
    row = lax.broadcasted_iota(jnp.int32, (128, 256), 0)
    lane = lax.broadcasted_iota(jnp.int32, (128, 256), 1)
    return row % 8 == lane % 8


def halo_copies(ext, send, recv, b, before, after):
    return (
        remote(ext.at[9:16], ext.at[1:8], send.at[0, b], recv.at[0, b], after),
        remote(ext.at[8:15], ext.at[16:23], send.at[1, b], recv.at[1, b], before),
    )


def return_copies(out, back, send, recv, b, before, after):
    return (
        remote(out.at[0:7], back.at[8:15], send.at[0, b], recv.at[0, b], before),
        remote(out.at[9:16], back.at[1:8], send.at[1, b], recv.at[1, b], after),
    )


def column_shifts(flat):
    count = flat.shape[0]
    col = lax.broadcasted_iota(jnp.int32, flat.shape, 0) % COLS
    left = jnp.where(col == 0, 0.0, pltpu.roll(flat, 1, 0))
    right = jnp.where(col == COLS - 1, 0.0, pltpu.roll(flat, count - 1, 0))
    return left, right


ORDERS = (("x", "y", "z"), ("y", "z", "x"), ("z", "x", "y"))


def place_of(tm, row):
    return {"y": tm // 8, "x": (row // 2) * 2 + (tm // 4) % 2, "z": tm % 4, "core": row % 2}


def device_at(at):
    return (at["y"] * 8 + (at["x"] % 2) * 4 + at["z"], (at["x"] // 2) * 2 + at["core"])


def cell_groups(block):
    wide = block.astype(F32)
    return [wide[:, 8 * g : 8 * g + 8].reshape(128, wide.shape[2]) for g in range(2)]


def from_groups(rows):
    return jnp.concatenate(
        [rows[128 * g : 128 * g + 128].reshape(16, 8, rows.shape[1]) for g in range(2)], axis=1
    )


def scratch_list():
    dma = pltpu.SemaphoreType.DMA
    plane = VMEM((FR, COLS, CH), BF)
    tile = (16, 128)
    return {
        "wo32": VMEM((PADQ, CH), F32),
        "wp": VMEM((CH, PADZ), BF),
        "wop": VMEM((PADQ, CH), BF),
        **{f"hext{b}": VMEM((24, BC, CH), BF) for b in range(4)},
        **{f"wout{b}": VMEM((16, BC, CH), BF) for b in range(4)},
        **{f"back{b}": VMEM((16, BC, CH), BF) for b in range(4)},
        **{f"cext{b}": VMEM((24, BC, CH), BF) for b in range(4)},
        **{f"dh{b}": VMEM((16, BC, CH), BF) for b in range(4)},
        **{f"dback{b}": VMEM((16, BC, CH), BF) for b in range(4)},
        "z": VMEM((1024, PADZ), BF),
        "hall": VMEM((1024, 384), BF),
        "mall": VMEM((1024, PADQ), BF),
        "call": VMEM((1024, CH), BF),
        "dz": VMEM((1024, PADZ), BF),
        "pt": VMEM((32, 256, 128), BF),
        "motion": VMEM((FR, CELLS, CH), BF),
        "normed": VMEM((FR, CELLS, CH), BF),
        "dmot": VMEM((FR, CELLS, CH), F32),
        "wbuf": VMEM((3, 1024, HID), BF),
        "x3": VMEM((FR, 4, COLS, 1024), BF),
        "top": plane,
        "bot": plane,
        "pre": VMEM((FR * CELLS, HID), F32),
        "dpre": VMEM((FR * CELLS, HID), BF),
        "gtop": plane,
        "gbot": plane,
        "stop": plane,
        "sbot": plane,
        "keep": VMEM((FR, 2, COLS, CH), F32),
        **{f"flat{j}": VMEM((1608, 128), F32) for j in range(3)},
        **{f"a0{j}": VMEM((2, 64) + tile, BF) for j in range(3)},
        **{f"r0{j}": VMEM((64,) + tile, BF) for j in range(3)},
        **{f"a1{j}": VMEM((64,) + tile, BF) for j in range(3)},
        **{f"r1{j}": VMEM((3, 16) + tile, BF) for j in range(3)},
        **{f"a2{j}": VMEM((16,) + tile, BF) for j in range(3)},
        **{f"r2{j}": VMEM((3, 4) + tile, BF) for j in range(3)},
        **{f"a3{j}": VMEM((4,) + tile, BF) for j in range(3)},
        **{f"r3{j}": VMEM((3, 1) + tile, BF) for j in range(3)},
        "wsem": dma((18,)),
        **{name: dma((2, 4)) for name in ("s1", "q1", "s2", "q2", "s3", "q3", "s4", "q4")},
        "srow": dma((4,)),
        "qrow": dma((4,)),
        "ssum": dma((3, 10)),
        "qsum": dma((3, 10)),
    }


def step_kernel(
    shift_ref, lat_ref, mgain_ref, sgain_ref, emb_ref, tw_ref, w_ref, wo_ref, conv_ref, projt_ref, cot_ref,
    out_ref, gin_ref, sum_ref, *rest,
):
    m = dict(zip(scratch_list(), rest))
    blocks = {name: [m[f"{name}{b}"] for b in range(4)] for name in ("hext", "wout", "back", "cext", "dh", "dback")}
    wp, wop, wbuf, x3, dpre = m["wp"], m["wop"], m["wbuf"], m["x3"], m["dpre"]
    tm, row = lax.axis_index("tm"), lax.axis_index("row")
    rows = lax.axis_size("row")
    before, after = ring()
    above, below = (tm, row - 1), (tm, row + 1)
    has_above, has_below = row > 0, row < rows - 1
    me = place_of(tm, row)
    twin = device_at({**me, "core": 1 - me["core"]})
    peers = {
        axis: [device_at({**me, axis: (me[axis] + d) % 4}) for d in (1, 2, 3)] for axis in "xyz"
    }
    shift = shift_ref[0]
    mgain, sgain = mgain_ref[...].reshape(1, CH), sgain_ref[...].reshape(1, CH)

    loads = []
    for dy in (1, 0, 2):
        for t in range(3):
            loads.append((conv_ref.at[3 * dy + t, 0:256, :], wbuf.at[dy, 256 * t : 256 * t + 256, :]))
            loads.append((conv_ref.at[3 * dy + t, 256:320, :], wbuf.at[dy, 768 + 64 * t : 832 + 64 * t, :]))
    loads = [pltpu.make_async_copy(a, c, m["wsem"].at[j]) for j, (a, c) in enumerate(loads)]
    for load in loads:
        load.start()

    for b in range(BLOCKS):
        x = lat_ref[:, BC * b : BC * b + BC, :].astype(F32)
        blocks["hext"][b][8:16] = (x * rms_scale(x) * mgain).astype(BF)
    greet(
        (before, after, (tm, (row + 1) % rows), (tm, (row + rows - 1) % rows), twin)
        + tuple(peers["x"] + peers["y"] + peers["z"])
    )
    sends = []

    def start(*copies):
        for copy in copies:
            copy.start()
        sends.extend(copies)
        return copies

    def halos(name, send, recv):
        return [
            start(*halo_copies(blocks[name][b], m[send], m[recv], b, before, after))
            for b in range(BLOCKS)
        ]

    def arrive(pair):
        for copy in pair:
            copy.wait_recv()

    ins = halos("hext", "s1", "q1")
    wp[...] = jnp.zeros_like(wp)
    for j in range(3 * HEADS):
        wp[:, HP * j : HP * j + HD] = w_ref[:, HD * j : HD * j + HD]
    m["wo32"][...] = jnp.zeros_like(m["wo32"])
    wo_f = wo_ref[...].astype(F32)
    for h in range(HEADS):
        m["wo32"][HP * h : HP * h + HD, :] = wo_f[HD * h : HD * h + HD]
    wop[...] = m["wo32"][...].astype(BF)
    emb = emb_ref[...]
    three = stack_parts(emb)
    extra = sum(mm(three, part.astype(BF)) for part in parts_of(tw_ref[...]))
    extra = jnp.sum(extra, axis=0, keepdims=True)
    off = jnp.sum(mm(stack_parts(extra), wp[...]), axis=0, keepdims=True)
    for dy in range(3):
        wbuf[dy, 960:1024, :] = jnp.zeros((64, HID), BF)
    first, same = pair_masks(), same_cell()
    same_t = (
        lax.broadcasted_iota(jnp.int32, (256, 128), 0) % 8
        == lax.broadcasted_iota(jnp.int32, (256, 128), 1) % 8
    )
    lane = lax.broadcasted_iota(jnp.int32, (256, 64), 1)
    ones = jnp.where(lane == 0, 1.0, 0.0).astype(BF)

    def z_pair(g, i, part):
        return m["z"][128 * g : 128 * g + 128, PADQ * part + 128 * i : PADQ * part + 128 * i + 128]

    outs = []
    for b in range(BLOCKS):
        arrive(ins[b])
        for g, found in enumerate(cell_groups(blocks["hext"][b][pl.ds(shift, 16)])):
            m["hall"][256 * b + 128 * g : 256 * b + 128 * g + 128, 0:CH] = found.astype(BF)
        m["hall"][256 * b : 256 * b + 256, CH:384] = ones
        m["z"][256 * b : 256 * b + 256, :] = (
            mm(m["hall"][256 * b : 256 * b + 256, 0:CH], wp[...]) + off
        ).astype(BF)
        for g in (2 * b, 2 * b + 1):
            for i in range(HEADS // 2):
                p = pair_probs(z_pair(g, i, 0), both_heads(z_pair(g, i, 1), first), same).astype(BF)
                m["mall"][128 * g : 128 * g + 128, 128 * i : 128 * i + 128] = mm(
                    p, both_heads(z_pair(g, i, 2), first)
                ).astype(BF)
        found = mm(m["mall"][256 * b : 256 * b + 256, :], wop[...])
        blocks["wout"][b][...] = from_groups(found).astype(BF)
        outs.append(
            start(*return_copies(blocks["wout"][b], blocks["back"][b], m["s2"], m["q2"], b, before, after))
        )

    def transposed_probs(b):
        for g in (2 * b, 2 * b + 1):
            for i in range(HEADS // 2):
                s = mm_nt(both_heads(z_pair(g, i, 1), first), z_pair(g, i, 0))
                e = jnp.where(same_t, jnp.exp2(s * EXP2), 0.0)
                ea, eb = e[:128], e[128:]
                ea = ea * (1.0 / jnp.sum(ea, axis=0, keepdims=True))
                eb = eb * (1.0 / jnp.sum(eb, axis=0, keepdims=True))
                m["pt"][4 * g + i, 0:128] = ea.astype(BF)
                m["pt"][4 * g + i, 128:256] = eb.astype(BF)

    transposed_probs(0)
    transposed_probs(1)

    up = remote(m["normed"].at[:, 0:32, :], m["bot"], m["srow"].at[0], m["qrow"].at[0], above)
    down = remote(m["normed"].at[:, 32:64, :], m["top"], m["srow"].at[1], m["qrow"].at[1], below)
    gup = remote(m["stop"], m["gbot"], m["srow"].at[2], m["qrow"].at[2], above)
    gdown = remote(m["sbot"], m["gtop"], m["srow"].at[3], m["qrow"].at[3], below)
    for b in range(BLOCKS):
        arrive(outs[b])
        x = lat_ref[:, BC * b : BC * b + BC, :].astype(F32)
        both = blocks["wout"][b][pl.ds(8 - shift, 8)].astype(F32)
        both = both + blocks["back"][b][pl.ds(8 - shift, 8)].astype(F32)
        moved = (x + 0.5 * both).astype(BF)
        m["motion"][:, BC * b : BC * b + BC, :] = moved
        moved = moved.astype(F32)
        m["normed"][:, BC * b : BC * b + BC, :] = (moved * rms_scale(moved) * sgain).astype(BF)
        if b == 1:
            pl.when(has_above)(lambda: up.start())
        if b == 3:
            pl.when(has_below)(lambda: down.start())

    def place(at, plane):
        flat = plane.astype(F32).reshape(FR * COLS, CH)
        left, right = column_shifts(flat)
        for t, values in enumerate((left, flat, right)):
            values = values.astype(BF).reshape(FR, COLS, CH)
            x3[:, at, :, 256 * t : 256 * t + 256] = values[:, :, :256]
            x3[:, at, :, 768 + 64 * t : 832 + 64 * t] = values[:, :, 256:]
        x3[:, at, :, 960:1024] = jnp.zeros((FR, COLS, 64), BF)

    place(1, m["normed"][:, 0:32, :])
    place(2, m["normed"][:, 32:64, :])

    def add_taps(dy, n):
        taps = x3[:, dy : dy + 2].reshape(FR * CELLS, 1024)
        return mm(taps, wbuf[dy, :, 256 * n : 256 * n + 256])

    for load in loads[:6]:
        load.wait()
    for n in range(5):
        m["pre"][:, 256 * n : 256 * n + 256] = add_taps(1, n)

    @pl.when(has_below)
    def _():
        remote(m["normed"].at[:, 0:32, :], m["bot"], m["srow"].at[0], m["qrow"].at[0], below).wait_recv()
        place(3, m["bot"][...])

    @pl.when(jnp.logical_not(has_below))
    def _():
        x3[:, 3] = jnp.zeros((FR, COLS, 1024), BF)

    @pl.when(has_above)
    def _():
        remote(m["normed"].at[:, 32:64, :], m["top"], m["srow"].at[1], m["qrow"].at[1], above).wait_recv()
        place(0, m["top"][...])

    @pl.when(jnp.logical_not(has_above))
    def _():
        x3[:, 0] = jnp.zeros((FR, COLS, 1024), BF)

    for load in loads[6:]:
        load.wait()
    cot = cot_ref[...].reshape(FR * CELLS, CH)
    total = m["motion"][...].astype(F32).reshape(FR * CELLS, CH)
    c0, c1 = math.sqrt(2.0 / math.pi), 0.044715
    for n in range(5):
        u = m["pre"][:, 256 * n : 256 * n + 256] + add_taps(0, n) + add_taps(2, n)
        proj = projt_ref[:, 256 * n : 256 * n + 256]
        dact = mm(cot, proj)
        sq = u * u
        th = jnp.tanh(c0 * u * (1.0 + c1 * sq))
        half = 0.5 + 0.5 * th
        act = u * half
        slope = half + 0.5 * u * (1.0 - th * th) * (c0 + (3.0 * c0 * c1) * sq)
        dpre[:, 256 * n : 256 * n + 256] = (slope * dact).astype(BF)
        total = total + mm_nt(act.astype(BF), proj)
    out_ref[...] = total.astype(BF).reshape(FR, CELLS, CH)

    def back_taps(dy):
        g = [mm_nt(dpre[...], wbuf[dy, 256 * j : 256 * j + 256, :]) for j in range(4)]
        col = lax.broadcasted_iota(jnp.int32, (FR * CELLS, 256), 0) % COLS
        count = FR * CELLS

        def from_right(x, c):
            return jnp.where(c == COLS - 1, 0.0, pltpu.roll(x, count - 1, 0))

        def from_left(x, c):
            return jnp.where(c == 0, 0.0, pltpu.roll(x, 1, 0))

        low = from_right(g[0], col) + g[1] + from_left(g[2], col)
        high = (
            from_right(g[3][:, :64], col[:, :64])
            + g[3][:, 64:128]
            + from_left(g[3][:, 128:192], col[:, :64])
        )
        return jnp.concatenate([low, high], axis=1).reshape(FR, 2, COLS, CH)

    keep = m["keep"]
    y = back_taps(0)
    m["stop"][...] = y[:, 0].astype(BF)
    pl.when(has_above)(lambda: gup.start())
    keep[:, 0] = y[:, 1]
    y = back_taps(2)
    m["sbot"][...] = y[:, 1].astype(BF)
    pl.when(has_below)(lambda: gdown.start())
    keep[:, 1] = y[:, 0]
    keep[...] = keep[...] + back_taps(1)

    def row_cotangent(r):
        cells = slice(32 * r, 32 * r + 32)
        d = cot_ref[:, cells, :].astype(F32) + rms_back(
            m["motion"][:, cells, :].astype(F32), sgain, keep[:, r]
        )
        m["dmot"][:, cells, :] = d
        d = (0.5 * d).astype(BF)
        for b in (2 * r, 2 * r + 1):
            blocks["cext"][b][8:16] = d[:, BC * (b - 2 * r) : BC * (b - 2 * r) + BC]

    @pl.when(has_above)
    def _():
        remote(m["sbot"], m["gtop"], m["srow"].at[3], m["qrow"].at[3], above).wait_recv()
        keep[:, 0] = keep[:, 0] + m["gtop"][...].astype(F32)

    row_cotangent(0)

    def send_halo(b):
        return start(*halo_copies(blocks["cext"][b], m["s3"], m["q3"], b, before, after))

    ins = [send_halo(0), send_halo(1)]

    @pl.when(has_below)
    def _():
        remote(m["stop"], m["gbot"], m["srow"].at[2], m["qrow"].at[2], below).wait_recv()
        keep[:, 1] = keep[:, 1] + m["gbot"][...].astype(F32)

    row_cotangent(1)
    ins += [send_halo(2), send_halo(3)]

    transposed_probs(2)
    transposed_probs(3)
    outs = []
    for b in range(BLOCKS):
        arrive(ins[b])
        for g, found in enumerate(cell_groups(blocks["cext"][b][pl.ds(shift, 16)])):
            m["call"][256 * b + 128 * g : 256 * b + 128 * g + 128, :] = found.astype(BF)
        dm = mm_nt(m["call"][256 * b : 256 * b + 256, :], wop[...]).astype(BF)
        for g in (2 * b, 2 * b + 1):
            at = slice(128 * g, 128 * g + 128)
            for i in range(HEADS // 2):
                lanes = slice(128 * i, 128 * i + 128)
                q = z_pair(g, i, 0)
                kst = both_heads(z_pair(g, i, 1), first)
                vst = both_heads(z_pair(g, i, 2), first)
                dmi = dm[128 * (g - 2 * b) : 128 * (g - 2 * b) + 128, lanes]
                pt = m["pt"][4 * g + i]
                pf = pt.astype(F32)
                dp = mm_nt(vst, dmi)
                t = pf * dp
                ds = jnp.concatenate(
                    [
                        (t[:128] - pf[:128] * jnp.sum(t[:128], axis=0, keepdims=True)) * SCALE,
                        (t[128:] - pf[128:] * jnp.sum(t[128:], axis=0, keepdims=True)) * SCALE,
                    ],
                    axis=0,
                ).astype(BF)
                m["dz"][at, lanes] = mm_tn(ds, kst).astype(BF)
                dk = mm(ds, q)
                m["dz"][at, PADQ + 128 * i : PADQ + 128 * i + 128] = jnp.where(
                    first, dk[:128], dk[128:]
                ).astype(BF)
                dv = mm(pt, dmi)
                m["dz"][at, 2 * PADQ + 128 * i : 2 * PADQ + 128 * i + 128] = jnp.where(
                    first, dv[:128], dv[128:]
                ).astype(BF)
        found = mm_nt(m["dz"][256 * b : 256 * b + 256, :], wp[...])
        blocks["dh"][b][...] = from_groups(found).astype(BF)
        outs.append(
            start(*return_copies(blocks["dh"][b], blocks["dback"][b], m["s4"], m["q4"], b, before, after))
        )

    flats = [m[f"flat{j}"] for j in range(3)]
    dw = mm_tn(m["hall"][...], m["dz"][...])
    doff = dw[CH : CH + 1]
    dwq = dw[:CH] + outer(extra, doff)
    at = lax.broadcasted_iota(jnp.int32, (PADQ, 384), 0)
    lane = lax.broadcasted_iota(jnp.int32, (PADQ, 384), 1)
    pick = (lane == HD * (at // HP) + at % HP) & (at % HP < HD)
    pick = jnp.where(pick, 1.0, 0.0).astype(BF)
    for part in range(3):
        block = mm(dwq[:, PADQ * part : PADQ * part + PADQ].astype(BF), pick)
        for j in range(3):
            flats[j][pl.ds(part, CH, stride=3), :] = block[:, 128 * j : 128 * j + 128]
    zeros = jnp.zeros((CH, 64), F32)
    dwo = mm_tn(m["mall"][...], m["call"][...])
    dext = jnp.sum(mm_nt(stack_parts(doff), wp[...]), axis=0, keepdims=True)
    dtime = outer(emb, dext)
    for j in range(3):
        wide = 128 if j < 2 else 64
        for h in range(HEADS):
            flats[j][960 + HD * h : 960 + HD * h + HD, 0:wide] = dwo[
                HP * h : HP * h + HD, 128 * j : 128 * j + wide
            ]
        flats[j][1280:1600, 0:wide] = dtime[:, 128 * j : 128 * j + wide]
        flats[j][1600:1608, :] = jnp.zeros((8, 128), F32)
    flats[2][960:1280, 64:128] = zeros
    flats[2][1280:1600, 64:128] = zeros

    a = [[m[f"a{k}{j}"] for j in range(3)] for k in range(4)]
    r = [[m[f"r{k}{j}"] for j in range(3)] for k in range(4)]

    def gather(j, carry):
        to = place_of(j // 2, (j % 2) * 2)
        for c in range(2):
            for part, order in enumerate(ORDERS):
                index = (to[order[0]] * 4 + to[order[1]]) * 4 + to[order[2]]
                a[0][part][c, index] = flats[part][pl.ds(25 * j + 12 * c, 16), :].astype(BF)
        return carry

    lax.fori_loop(0, 64, gather, 0)
    core = me["core"]
    stage = [
        start(
            remote(a[0][p].at[1 - core], r[0][p], m["ssum"].at[p, 0], m["qsum"].at[p, 0], twin)
        )
        for p in range(3)
    ]

    def fan_out(part, level):
        axis = ORDERS[part][level - 1]
        step = 16 >> (2 * (level - 1))
        copies = []
        for d in range(3):
            to = (me[axis] + d + 1) % 4
            sem = 3 * level - 2 + d
            copies.append(
                remote(
                    a[level][part].at[pl.ds(to * step, step)], r[level][part].at[d],
                    m["ssum"].at[part, sem], m["qsum"].at[part, sem], peers[axis][d],
                )
            )
        return start(*copies)

    def gathered(part, level):
        step = 16 >> (2 * (level - 1))
        own = me[ORDERS[part][level - 1]]
        total = a[level][part][pl.ds(own * step, step)].astype(F32)
        for d in range(3):
            total = total + r[level][part][d].astype(F32)
        return total

    def finish(b):
        arrive(outs[b])
        d_hidden = blocks["dh"][b][pl.ds(8 - shift, 8)].astype(F32)
        d_hidden = d_hidden + blocks["dback"][b][pl.ds(8 - shift, 8)].astype(F32)
        x = lat_ref[:, BC * b : BC * b + BC, :].astype(F32)
        gin_ref[:, BC * b : BC * b + BC, :] = m["dmot"][:, BC * b : BC * b + BC, :] + rms_back(
            x, mgain, d_hidden
        )

    finish(0)
    for p in range(3):
        arrive(stage[p])
        a[1][p][...] = (a[0][p][core].astype(F32) + r[0][p][...].astype(F32)).astype(BF)
        stage[p] = fan_out(p, 1)
    finish(1)
    finish(2)
    finish(3)
    for level in (2, 3):
        for p in range(3):
            arrive(stage[p])
            a[level][p][...] = gathered(p, level - 1).astype(BF)
            stage[p] = fan_out(p, level)
    for p in range(3):
        arrive(stage[p])
        sum_ref[:, 128 * p : 128 * p + 128] = gathered(p, 3)[0] * (1.0 / 256.0)
    for copy in sends:
        copy.wait_send()

    @pl.when(has_above)
    def _():
        up.wait_send()
        gup.wait_send()

    @pl.when(has_below)
    def _():
        down.wait_send()
        gdown.wait_send()


def embedding(timestep_ids, channels):
    half_width = channels // 2
    frequency = jnp.exp(-math.log(10000.0) * jnp.arange(half_width, dtype=F32) / half_width)
    angles = timestep_ids.astype(F32)[:, None] * frequency[None, :]
    return jnp.concatenate([jnp.cos(angles), jnp.sin(angles)], axis=-1)


def vmem(count):
    return [pl.BlockSpec(memory_space=VMEM)] * count


def params(ident):
    return pltpu.CompilerParams(
        collective_id=ident, has_side_effects=True, vmem_limit_bytes=VLIM
    )


def shaped(*shape, dtype=BF):
    return jax.ShapeDtypeStruct(shape, dtype)


def on_device(
    latents,
    window_shift,
    timesteps,
    motion_gain,
    time_weight,
    qkv_weight,
    attn_out_weight,
    spatial_gain,
    conv_weight,
    proj_weight,
    out_cotangent,
):
    smem = pl.BlockSpec(memory_space=pltpu.SMEM)
    block_output, grad_input, total = pl.pallas_call(
        step_kernel,
        out_shape=(
            shaped(FR, CELLS, CH), shaped(FR, CELLS, CH, dtype=F32), shaped(16, 384, dtype=F32),
        ),
        in_specs=[smem] + vmem(7) + [pl.BlockSpec(memory_space=pl.ANY)] + vmem(2),
        out_specs=tuple(vmem(3)),
        scratch_shapes=list(scratch_list().values()),
        compiler_params=params(0),
        name="step",
    )(
        window_shift, latents.reshape(FR, CELLS, CH), motion_gain, spatial_gain,
        embedding(timesteps, CH), time_weight, qkv_weight, attn_out_weight, conv_weight,
        proj_weight.T, out_cotangent.reshape(FR, CELLS, CH),
    )
    odd = lax.axis_index("row") % 2
    grad_weights = lax.dynamic_slice_in_dim(total[:13, :CH].reshape(-1), 160 * odd, 4000)
    return (
        block_output.reshape(latents.shape),
        grad_input.reshape(latents.shape),
        grad_weights,
    )


def solution(mesh):
    placed = (
        P("tm", "row", None, None),
        P(),
        P("tm"),
        P(),
        P(),
        P(),
        P(),
        P(),
        P(),
        P(),
        P("tm", "row", None, None),
    )
    return jax.shard_map(
        on_device,
        mesh=mesh,
        in_specs=placed,
        out_specs=(P("tm", "row", None, None), P("tm", "row", None, None), P(("tm", "row"))),
        check_vma=False,
    )
```

profile of v0, /device:TPU:0, one launch (start us, length us, event | category | flops | bytes accessed | tf_op | source)
XLA Modules:
  0.0 91.0 jit_solution(5077668165319245352)
XLA Ops:
  1.3 0.1 fusion
  1.4 0.6 pad_maximum_fusion.emb_ref
  2.6 83.0 %step.1 = (bf16[8,64,320]{2,1,0:T(8,128)(2,1)}, f32[8,64,320]{2,1,0:T(8,128)}, f32[16,384]{1,0:T(8,128)}) custom-call(s32[1]{0:T(128)S(6)} %copy.16.shift_ref, bf16[8,64,320]{2,1,0:T(8,128)(2,1)} %bitcast.10, f32[320]{0:T(512)} %mgain_ref.1, f32[320]{0:T(512)} %sgain_ref.1, f32[1,320]{1,0:T(1,128)} %pad_maximum_fusion.emb_ref, f32[320,320]{1,0:T(8,128)} %tw_ref.1, ...), custom_call_target="tpu_custom_call" | custom-call | tf_op jit(solution)/shard_map/step/pallas_call | solution.py:659
  85.6 0.8 reshape.51
  86.4 0.7 dynamic_slice.3
  87.1 1.8 %copy.18 = bf16[8,2,32,320]{3,2,1,0:T(8,128)(2,1)} copy(bf16[8,2,32,320]{3,2,1,0:T(8,128)(2,1)} %bitcast.9) | data formatting | bytes 655360
  88.9 2.1 %copy.19 = f32[8,2,32,320]{3,2,1,0:T(8,128)} copy(f32[8,2,32,320]{3,2,1,0:T(8,128)} %bitcast.8) | data formatting | bytes 1310720
where the time goes:
time: 91.5 us; the launch traced here: 91 us
  Pallas kernels  83 us (91%)
  local copies, waits for them, and re-layouts  5.34 us (6%)
  between operations  1.96 us (2%)
    pallas_call x1, Pallas kernels, on_device(): pl.pallas_call(step_kernel, out_shape=(shaped(FR, CELLS, CH), shaped(FR,...  83 us
    unnamed x2, local copies, waits for them, and re-layouts  3.85 us

commit v1 on v0

--- a/solution.py
+++ b/solution.py
@@ -27,7 +27,7 @@
 SCALE = 1.0 / math.sqrt(HD)
 EXP2 = SCALE * math.log2(math.e)
 EPS = 1e-06
-VLIM = 56 * 1024 * 1024
+VLIM = 60 * 1024 * 1024
 
 
 def mm(a, b):
@@ -75,11 +75,9 @@
     return mm_tn(lhs, rhs)
 
 
-def greet(peers):
-    barrier = pltpu.get_barrier_semaphore()
+def greet(barrier, peers):
     for peer in peers:
         pl.semaphore_signal(barrier, inc=1, device_id=peer, device_id_type=MESH)
-    pl.semaphore_wait(barrier, len(peers))
 
 
 def remote(src, dst, send, recv, peer):
@@ -165,6 +163,43 @@
     return jnp.concatenate(
         [rows[128 * g : 128 * g + 128].reshape(16, 8, rows.shape[1]) for g in range(2)], axis=1
     )
+
+
+def flat_line(sums, line, half):
+    lane = lax.broadcasted_iota(jnp.int32, (8, 128), 1)
+    even = [sums[p, pl.ds(0, 8, stride=2), :] for p in range(3)]
+    odd = [sums[p, pl.ds(1, 8, stride=2), :] for p in range(3)]
+    turned = [pltpu.roll(x, 64, 1) for x in odd]
+    low = lane < 64
+    pieces = (
+        even[0],
+        even[1],
+        jnp.where(low, even[2], turned[0]),
+        jnp.where(low, turned[0], turned[1]),
+        jnp.where(low, turned[1], turned[2]),
+    )
+    line[40:48, :] = jnp.zeros((8, 128), F32)
+    for j, piece in enumerate(pieces):
+        line[pl.ds(j, 8, stride=5), :] = piece
+    lane = lax.broadcasted_iota(jnp.int32, (32, 128), 1)
+    later = jnp.where(
+        lane < 96, pltpu.roll(line[1:33, :], 96, 1), pltpu.roll(line[2:34, :], 96, 1)
+    )
+    return jnp.where(half, later, line[0:32, :])
+
+
+def copy_kernel(out_in, gin_in, line_in, out_ref, gin_ref, line_ref, sems):
+    copies = [
+        pltpu.make_async_copy(out_in, out_ref, sems.at[0]),
+        pltpu.make_async_copy(gin_in, gin_ref, sems.at[1]),
+    ]
+    for copy in copies:
+        copy.start()
+    for j in range(31):
+        line_ref[128 * j : 128 * j + 128] = line_in[j]
+    line_ref[3968:4000] = line_in[31, 0:32]
+    for copy in copies:
+        copy.wait()
 
 
 def scratch_list():
@@ -210,6 +245,18 @@
         **{f"r2{j}": VMEM((3, 4) + tile, BF) for j in range(3)},
         **{f"a3{j}": VMEM((4,) + tile, BF) for j in range(3)},
         **{f"r3{j}": VMEM((3, 1) + tile, BF) for j in range(3)},
+        "dact": VMEM((FR * CELLS, HID), F32),
+        "hallt": VMEM((384, 1024), BF),
+        "mallt": VMEM((PADQ, 1024), BF),
+        "pick": VMEM((PADQ, 384), BF),
+        "tw": VMEM((CH, CH), F32),
+        "w": VMEM((CH, 3 * CH), BF),
+        "wo": VMEM((CH, CH), BF),
+        "projt": VMEM((CH, HID), BF),
+        "cot": VMEM((FR, CELLS, CH), BF),
+        "line": VMEM((48, 128), F32),
+        "sums": VMEM((3, 16, 128), F32),
+        "osem": dma((5,)),
         "wsem": dma((18,)),
         **{name: dma((2, 4)) for name in ("s1", "q1", "s2", "q2", "s3", "q3", "s4", "q4")},
         "srow": dma((4,)),
@@ -220,7 +267,7 @@
 
 
 def step_kernel(
-    shift_ref, lat_ref, mgain_ref, sgain_ref, emb_ref, tw_ref, w_ref, wo_ref, conv_ref, projt_ref, cot_ref,
+    shift_ref, lat_ref, mgain_ref, sgain_ref, emb_ref, tw_hbm, w_hbm, wo_hbm, conv_ref, projt_hbm, cot_hbm,
     out_ref, gin_ref, sum_ref, *rest,
 ):
     m = dict(zip(scratch_list(), rest))
@@ -239,6 +286,17 @@
     shift = shift_ref[0]
     mgain, sgain = mgain_ref[...].reshape(1, CH), sgain_ref[...].reshape(1, CH)
 
+    barrier = pltpu.get_barrier_semaphore()
+    neighbours = (before, after, (tm, (row + 1) % rows), (tm, (row + rows - 1) % rows), twin)
+    neighbours += tuple(peers["x"] + peers["y"] + peers["z"])
+    greet(barrier, neighbours)
+    small = {}
+    for j, (name, ref) in enumerate(
+        (("w", w_hbm), ("wo", wo_hbm), ("tw", tw_hbm), ("cot", cot_hbm), ("projt", projt_hbm))
+    ):
+        small[name] = pltpu.make_async_copy(ref, m[name], m["osem"].at[j])
+        small[name].start()
+    w_ref, wo_ref, tw_ref, cot_ref, projt_ref = (m[k] for k in ("w", "wo", "tw", "cot", "projt"))
     loads = []
     for dy in (1, 0, 2):
         for t in range(3):
@@ -251,10 +309,7 @@
     for b in range(BLOCKS):
         x = lat_ref[:, BC * b : BC * b + BC, :].astype(F32)
         blocks["hext"][b][8:16] = (x * rms_scale(x) * mgain).astype(BF)
-    greet(
-        (before, after, (tm, (row + 1) % rows), (tm, (row + rows - 1) % rows), twin)
-        + tuple(peers["x"] + peers["y"] + peers["z"])
-    )
+    pl.semaphore_wait(barrier, len(neighbours))
     sends = []
 
     def start(*copies):
@@ -274,14 +329,17 @@
             copy.wait_recv()
 
     ins = halos("hext", "s1", "q1")
+    small["w"].wait()
     wp[...] = jnp.zeros_like(wp)
     for j in range(3 * HEADS):
         wp[:, HP * j : HP * j + HD] = w_ref[:, HD * j : HD * j + HD]
     m["wo32"][...] = jnp.zeros_like(m["wo32"])
+    small["wo"].wait()
     wo_f = wo_ref[...].astype(F32)
     for h in range(HEADS):
         m["wo32"][HP * h : HP * h + HD, :] = wo_f[HD * h : HD * h + HD]
     wop[...] = m["wo32"][...].astype(BF)
+    small["tw"].wait()
     emb = emb_ref[...]
     three = stack_parts(emb)
     extra = sum(mm(three, part.astype(BF)) for part in parts_of(tw_ref[...]))
@@ -294,6 +352,10 @@
         lax.broadcasted_iota(jnp.int32, (256, 128), 0) % 8
         == lax.broadcasted_iota(jnp.int32, (256, 128), 1) % 8
     )
+    at = lax.broadcasted_iota(jnp.int32, (PADQ, 384), 0)
+    lane = lax.broadcasted_iota(jnp.int32, (PADQ, 384), 1)
+    pick = (lane == HD * (at // HP) + at % HP) & (at % HP < HD)
+    m["pick"][...] = jnp.where(pick, 1.0, 0.0).astype(BF)
     lane = lax.broadcasted_iota(jnp.int32, (256, 64), 1)
     ones = jnp.where(lane == 0, 1.0, 0.0).astype(BF)
 
@@ -332,8 +394,15 @@
                 m["pt"][4 * g + i, 0:128] = ea.astype(BF)
                 m["pt"][4 * g + i, 128:256] = eb.astype(BF)
 
-    transposed_probs(0)
-    transposed_probs(1)
+    small["cot"].wait()
+    small["projt"].wait()
+    cot = cot_ref[...].reshape(FR * CELLS, CH)
+    for n in range(5):
+        m["dact"][:, 256 * n : 256 * n + 256] = mm(cot, projt_ref[:, 256 * n : 256 * n + 256])
+    m["hallt"][...] = m["hall"][...].T
+    m["mallt"][...] = m["mall"][...].T
+    transposed_probs(2)
+    transposed_probs(3)
 
     up = remote(m["normed"].at[:, 0:32, :], m["bot"], m["srow"].at[0], m["qrow"].at[0], above)
     down = remote(m["normed"].at[:, 32:64, :], m["top"], m["srow"].at[1], m["qrow"].at[1], below)
@@ -394,13 +463,12 @@
 
     for load in loads[6:]:
         load.wait()
-    cot = cot_ref[...].reshape(FR * CELLS, CH)
     total = m["motion"][...].astype(F32).reshape(FR * CELLS, CH)
     c0, c1 = math.sqrt(2.0 / math.pi), 0.044715
     for n in range(5):
         u = m["pre"][:, 256 * n : 256 * n + 256] + add_taps(0, n) + add_taps(2, n)
         proj = projt_ref[:, 256 * n : 256 * n + 256]
-        dact = mm(cot, proj)
+        dact = m["dact"][:, 256 * n : 256 * n + 256]
         sq = u * u
         th = jnp.tanh(c0 * u * (1.0 + c1 * sq))
         half = 0.5 + 0.5 * th
@@ -450,30 +518,37 @@
         for b in (2 * r, 2 * r + 1):
             blocks["cext"][b][8:16] = d[:, BC * (b - 2 * r) : BC * (b - 2 * r) + BC]
 
+    def send_halo(b):
+        return start(*halo_copies(blocks["cext"][b], m["s3"], m["q3"], b, before, after))
+
+    @pl.when(has_below)
+    def _():
+        remote(m["stop"], m["gbot"], m["srow"].at[2], m["qrow"].at[2], below).wait_recv()
+        keep[:, 1] = keep[:, 1] + m["gbot"][...].astype(F32)
+
+    row_cotangent(1)
+    ins = {b: send_halo(b) for b in (2, 3)}
+
     @pl.when(has_above)
     def _():
         remote(m["sbot"], m["gtop"], m["srow"].at[3], m["qrow"].at[3], above).wait_recv()
         keep[:, 0] = keep[:, 0] + m["gtop"][...].astype(F32)
 
     row_cotangent(0)
-
-    def send_halo(b):
-        return start(*halo_copies(blocks["cext"][b], m["s3"], m["q3"], b, before, after))
-
-    ins = [send_halo(0), send_halo(1)]
-
-    @pl.when(has_below)
-    def _():
-        remote(m["stop"], m["gbot"], m["srow"].at[2], m["qrow"].at[2], below).wait_recv()
-        keep[:, 1] = keep[:, 1] + m["gbot"][...].astype(F32)
-
-    row_cotangent(1)
-    ins += [send_halo(2), send_halo(3)]
-
-    transposed_probs(2)
-    transposed_probs(3)
-    outs = []
-    for b in range(BLOCKS):
+    ins.update({b: send_halo(b) for b in (0, 1)})
+
+    transposed_probs(0)
+    transposed_probs(1)
+    outs = {}
+
+    def give_back(b):
+        found = mm_nt(m["dz"][256 * b : 256 * b + 256, :], wp[...])
+        blocks["dh"][b][...] = from_groups(found).astype(BF)
+        outs[b] = start(
+            *return_copies(blocks["dh"][b], blocks["dback"][b], m["s4"], m["q4"], b, before, after)
+        )
+
+    for b in (2, 3, 0, 1):
         arrive(ins[b])
         for g, found in enumerate(cell_groups(blocks["cext"][b][pl.ds(shift, 16)])):
             m["call"][256 * b + 128 * g : 256 * b + 128 * g + 128, :] = found.astype(BF)
@@ -506,26 +581,19 @@
                 m["dz"][at, 2 * PADQ + 128 * i : 2 * PADQ + 128 * i + 128] = jnp.where(
                     first, dv[:128], dv[128:]
                 ).astype(BF)
-        found = mm_nt(m["dz"][256 * b : 256 * b + 256, :], wp[...])
-        blocks["dh"][b][...] = from_groups(found).astype(BF)
-        outs.append(
-            start(*return_copies(blocks["dh"][b], blocks["dback"][b], m["s4"], m["q4"], b, before, after))
-        )
+        if b > 1:
+            give_back(b)
 
     flats = [m[f"flat{j}"] for j in range(3)]
-    dw = mm_tn(m["hall"][...], m["dz"][...])
+    dw = mm(m["hallt"][...], m["dz"][...])
     doff = dw[CH : CH + 1]
     dwq = dw[:CH] + outer(extra, doff)
-    at = lax.broadcasted_iota(jnp.int32, (PADQ, 384), 0)
-    lane = lax.broadcasted_iota(jnp.int32, (PADQ, 384), 1)
-    pick = (lane == HD * (at // HP) + at % HP) & (at % HP < HD)
-    pick = jnp.where(pick, 1.0, 0.0).astype(BF)
     for part in range(3):
-        block = mm(dwq[:, PADQ * part : PADQ * part + PADQ].astype(BF), pick)
+        block = mm(dwq[:, PADQ * part : PADQ * part + PADQ].astype(BF), m["pick"][...])
         for j in range(3):
             flats[j][pl.ds(part, CH, stride=3), :] = block[:, 128 * j : 128 * j + 128]
     zeros = jnp.zeros((CH, 64), F32)
-    dwo = mm_tn(m["mall"][...], m["call"][...])
+    dwo = mm(m["mallt"][...], m["call"][...])
     dext = jnp.sum(mm_nt(stack_parts(doff), wp[...]), axis=0, keepdims=True)
     dtime = outer(emb, dext)
     for j in range(3):
@@ -591,14 +659,14 @@
             x, mgain, d_hidden
         )
 
-    finish(0)
+    give_back(0)
+    give_back(1)
     for p in range(3):
         arrive(stage[p])
         a[1][p][...] = (a[0][p][core].astype(F32) + r[0][p][...].astype(F32)).astype(BF)
         stage[p] = fan_out(p, 1)
-    finish(1)
-    finish(2)
-    finish(3)
+    for b in (2, 3, 0, 1):
+        finish(b)
     for level in (2, 3):
         for p in range(3):
             arrive(stage[p])
@@ -606,7 +674,8 @@
             stage[p] = fan_out(p, level)
     for p in range(3):
         arrive(stage[p])
-        sum_ref[:, 128 * p : 128 * p + 128] = gathered(p, 3)[0] * (1.0 / 256.0)
+        m["sums"][p] = gathered(p, 3)[0] * (1.0 / 256.0)
+    sum_ref[...] = flat_line(m["sums"], m["line"], core == 1)
     for copy in sends:
         copy.wait_send()
 
@@ -630,6 +699,10 @@
 
 def vmem(count):
     return [pl.BlockSpec(memory_space=VMEM)] * count
+
+
+def anywhere(count):
+    return [pl.BlockSpec(memory_space=pl.ANY)] * count
 
 
 def params(ident):
@@ -659,9 +732,9 @@
     block_output, grad_input, total = pl.pallas_call(
         step_kernel,
         out_shape=(
-            shaped(FR, CELLS, CH), shaped(FR, CELLS, CH, dtype=F32), shaped(16, 384, dtype=F32),
+            VMEM((FR, CELLS, CH), BF), VMEM((FR, CELLS, CH), F32), VMEM((32, 128), F32),
         ),
-        in_specs=[smem] + vmem(7) + [pl.BlockSpec(memory_space=pl.ANY)] + vmem(2),
+        in_specs=[smem] + vmem(4) + anywhere(6),
         out_specs=tuple(vmem(3)),
         scratch_shapes=list(scratch_list().values()),
         compiler_params=params(0),
@@ -671,8 +744,17 @@
         embedding(timesteps, CH), time_weight, qkv_weight, attn_out_weight, conv_weight,
         proj_weight.T, out_cotangent.reshape(FR, CELLS, CH),
     )
-    odd = lax.axis_index("row") % 2
-    grad_weights = lax.dynamic_slice_in_dim(total[:13, :CH].reshape(-1), 160 * odd, 4000)
+    block_output, grad_input, grad_weights = pl.pallas_call(
+        copy_kernel,
+        out_shape=(
+            shaped(FR, CELLS, CH), shaped(FR, CELLS, CH, dtype=F32), shaped(4000, dtype=F32),
+        ),
+        in_specs=vmem(3),
+        out_specs=tuple(anywhere(2) + vmem(1)),
+        scratch_shapes=[pltpu.SemaphoreType.DMA((2,))],
+        compiler_params=pltpu.CompilerParams(vmem_limit_bytes=4 * 1024 * 1024),
+        name="results",
+    )(*(pltpu.with_memory_space_constraint(x, VMEM) for x in (block_output, grad_input, total)))
     return (
         block_output.reshape(latents.shape),
         grad_input.reshape(latents.shape),

time: 91.5 us -> 84.2 us (0.920)
  local copies, waits for them, and re-layouts: 5.34 us -> 0 us
  Pallas kernels: 83 us -> 81.2 us
    unnamed x2 -> x0, local copies, waits for them, and re-layouts: 3.85 us -> none
    pallas_call x1 -> x2, Pallas kernels: 83 us -> 81.2 us  [the longest x1 79.6 us: on_device(): pl.pallas_call(step_kernel, out_shape=(VMEM((FR, CELLS, CH), BF), VMEM((F...]
where the time goes in v1:
time: 84.2 us; the launch traced here: 84.1 us
  Pallas kernels  81.2 us (96%)
  between operations  2.12 us (3%)
    pallas_call x1, Pallas kernels, on_device(): pl.pallas_call(step_kernel, out_shape=(VMEM((FR, CELLS, CH), BF), VMEM((F...  79.6 us

profile of v1, /device:TPU:0, one launch (start us, length us, event | category | flops | bytes accessed | tf_op | source)
XLA Modules:
  0.0 84.1 jit_solution(7607720922065498406)
XLA Ops:
  1.9 0.1 fusion
  2.0 0.6 pad_maximum_fusion.emb_ref
  2.6 79.6 %step.1 = (bf16[8,64,320]{2,1,0:T(8,128)(2,1)S(1)}, f32[8,64,320]{2,1,0:T(8,128)S(1)}, f32[32,128]{1,0:T(8,128)S(1)}) custom-call(s32[1]{0:T(128)S(6)} %copy.14.shift_ref, bf16[8,64,320]{2,1,0:T(8,128)(2,1)} %bitcast.7, f32[320]{0:T(512)} %mgain_ref.1, f32[320]{0:T(512)} %sgain_ref.1, f32[1,320]{1,0:T(1,128)} %pad_maximum_fusion.emb_ref, f32[320,320]{1,0:T(8,128)} %tw_hbm.1, ...), custom_call_target="tpu_custom_call" | custom-call | tf_op jit(solution)/shard_map/step/pallas_call | solution.py:732
  82.2 1.6 %results.1 = (bf16[8,64,320]{2,1,0:T(8,128)(2,1)}, f32[8,64,320]{2,1,0:T(8,128)}, f32[4000]{0:T(1024)}) custom-call(bf16[8,64,320]{2,1,0:T(8,128)(2,1)S(1)} %get-tuple-element.9.out_in, f32[8,64,320]{2,1,0:T(8,128)S(1)} %get-tuple-element.10.gin_in, f32[32,128]{1,0:T(8,128)S(1)} %get-tuple-element.11.line_in), custom_call_target="tpu_custom_call" | custom-call | tf_op jit(solution)/shard_map/results/pallas_call | solution.py:747

commit v2 on v1

--- a/solution.py
+++ b/solution.py
@@ -21,7 +21,10 @@
 HD = 40
 HP = 64
 BLOCKS = 4
+HALF = BLOCKS // 2
 BC = CELLS // BLOCKS
+BG = BC // 8
+BR = 16 * BC
 PADQ = HEADS * HP
 PADZ = 3 * PADQ
 SCALE = 1.0 / math.sqrt(HD)
@@ -156,12 +159,12 @@
 
 def cell_groups(block):
     wide = block.astype(F32)
-    return [wide[:, 8 * g : 8 * g + 8].reshape(128, wide.shape[2]) for g in range(2)]
+    return [wide[:, 8 * g : 8 * g + 8].reshape(128, wide.shape[2]) for g in range(BG)]
 
 
 def from_groups(rows):
     return jnp.concatenate(
-        [rows[128 * g : 128 * g + 128].reshape(16, 8, rows.shape[1]) for g in range(2)], axis=1
+        [rows[128 * g : 128 * g + 128].reshape(16, 8, rows.shape[1]) for g in range(BG)], axis=1
     )
 
 
@@ -210,12 +213,12 @@
         "wo32": VMEM((PADQ, CH), F32),
         "wp": VMEM((CH, PADZ), BF),
         "wop": VMEM((PADQ, CH), BF),
-        **{f"hext{b}": VMEM((24, BC, CH), BF) for b in range(4)},
-        **{f"wout{b}": VMEM((16, BC, CH), BF) for b in range(4)},
-        **{f"back{b}": VMEM((16, BC, CH), BF) for b in range(4)},
-        **{f"cext{b}": VMEM((24, BC, CH), BF) for b in range(4)},
-        **{f"dh{b}": VMEM((16, BC, CH), BF) for b in range(4)},
-        **{f"dback{b}": VMEM((16, BC, CH), BF) for b in range(4)},
+        **{f"hext{b}": VMEM((24, BC, CH), BF) for b in range(BLOCKS)},
+        **{f"wout{b}": VMEM((16, BC, CH), BF) for b in range(BLOCKS)},
+        **{f"back{b}": VMEM((16, BC, CH), BF) for b in range(BLOCKS)},
+        **{f"cext{b}": VMEM((24, BC, CH), BF) for b in range(BLOCKS)},
+        **{f"dh{b}": VMEM((16, BC, CH), BF) for b in range(BLOCKS)},
+        **{f"dback{b}": VMEM((16, BC, CH), BF) for b in range(BLOCKS)},
         "z": VMEM((1024, PADZ), BF),
         "hall": VMEM((1024, 384), BF),
         "mall": VMEM((1024, PADQ), BF),
@@ -245,6 +248,7 @@
         **{f"r2{j}": VMEM((3, 4) + tile, BF) for j in range(3)},
         **{f"a3{j}": VMEM((4,) + tile, BF) for j in range(3)},
         **{f"r3{j}": VMEM((3, 1) + tile, BF) for j in range(3)},
+        "act": VMEM((FR * CELLS, HID), BF),
         "dact": VMEM((FR * CELLS, HID), F32),
         "hallt": VMEM((384, 1024), BF),
         "mallt": VMEM((PADQ, 1024), BF),
@@ -258,7 +262,7 @@
         "sums": VMEM((3, 16, 128), F32),
         "osem": dma((5,)),
         "wsem": dma((18,)),
-        **{name: dma((2, 4)) for name in ("s1", "q1", "s2", "q2", "s3", "q3", "s4", "q4")},
+        **{name: dma((2, BLOCKS)) for name in ("s1", "q1", "s2", "q2", "s3", "q3", "s4", "q4")},
         "srow": dma((4,)),
         "qrow": dma((4,)),
         "ssum": dma((3, 10)),
@@ -271,7 +275,7 @@
     out_ref, gin_ref, sum_ref, *rest,
 ):
     m = dict(zip(scratch_list(), rest))
-    blocks = {name: [m[f"{name}{b}"] for b in range(4)] for name in ("hext", "wout", "back", "cext", "dh", "dback")}
+    blocks = {name: [m[f"{name}{b}"] for b in range(BLOCKS)] for name in ("hext", "wout", "back", "cext", "dh", "dback")}
     wp, wop, wbuf, x3, dpre = m["wp"], m["wop"], m["wbuf"], m["x3"], m["dpre"]
     tm, row = lax.axis_index("tm"), lax.axis_index("row")
     rows = lax.axis_size("row")
@@ -356,35 +360,40 @@
     lane = lax.broadcasted_iota(jnp.int32, (PADQ, 384), 1)
     pick = (lane == HD * (at // HP) + at % HP) & (at % HP < HD)
     m["pick"][...] = jnp.where(pick, 1.0, 0.0).astype(BF)
-    lane = lax.broadcasted_iota(jnp.int32, (256, 64), 1)
+    lane = lax.broadcasted_iota(jnp.int32, (BR, 64), 1)
     ones = jnp.where(lane == 0, 1.0, 0.0).astype(BF)
 
     def z_pair(g, i, part):
         return m["z"][128 * g : 128 * g + 128, PADQ * part + 128 * i : PADQ * part + 128 * i + 128]
 
+    small["cot"].wait()
+    small["projt"].wait()
+    cot = cot_ref[...].reshape(FR * CELLS, CH)
+    for n in range(5):
+        m["dact"][:, 256 * n : 256 * n + 256] = mm(cot, projt_ref[:, 256 * n : 256 * n + 256])
     outs = []
     for b in range(BLOCKS):
         arrive(ins[b])
         for g, found in enumerate(cell_groups(blocks["hext"][b][pl.ds(shift, 16)])):
-            m["hall"][256 * b + 128 * g : 256 * b + 128 * g + 128, 0:CH] = found.astype(BF)
-        m["hall"][256 * b : 256 * b + 256, CH:384] = ones
-        m["z"][256 * b : 256 * b + 256, :] = (
-            mm(m["hall"][256 * b : 256 * b + 256, 0:CH], wp[...]) + off
+            m["hall"][BR * b + 128 * g : BR * b + 128 * g + 128, 0:CH] = found.astype(BF)
+        m["hall"][BR * b : BR * b + BR, CH:384] = ones
+        m["z"][BR * b : BR * b + BR, :] = (
+            mm(m["hall"][BR * b : BR * b + BR, 0:CH], wp[...]) + off
         ).astype(BF)
-        for g in (2 * b, 2 * b + 1):
+        for g in range(BG * b, BG * b + BG):
             for i in range(HEADS // 2):
                 p = pair_probs(z_pair(g, i, 0), both_heads(z_pair(g, i, 1), first), same).astype(BF)
                 m["mall"][128 * g : 128 * g + 128, 128 * i : 128 * i + 128] = mm(
                     p, both_heads(z_pair(g, i, 2), first)
                 ).astype(BF)
-        found = mm(m["mall"][256 * b : 256 * b + 256, :], wop[...])
+        found = mm(m["mall"][BR * b : BR * b + BR, :], wop[...])
         blocks["wout"][b][...] = from_groups(found).astype(BF)
         outs.append(
             start(*return_copies(blocks["wout"][b], blocks["back"][b], m["s2"], m["q2"], b, before, after))
         )
 
     def transposed_probs(b):
-        for g in (2 * b, 2 * b + 1):
+        for g in range(BG * b, BG * b + BG):
             for i in range(HEADS // 2):
                 s = mm_nt(both_heads(z_pair(g, i, 1), first), z_pair(g, i, 0))
                 e = jnp.where(same_t, jnp.exp2(s * EXP2), 0.0)
@@ -394,20 +403,24 @@
                 m["pt"][4 * g + i, 0:128] = ea.astype(BF)
                 m["pt"][4 * g + i, 128:256] = eb.astype(BF)
 
-    small["cot"].wait()
-    small["projt"].wait()
-    cot = cot_ref[...].reshape(FR * CELLS, CH)
-    for n in range(5):
-        m["dact"][:, 256 * n : 256 * n + 256] = mm(cot, projt_ref[:, 256 * n : 256 * n + 256])
     m["hallt"][...] = m["hall"][...].T
     m["mallt"][...] = m["mall"][...].T
-    transposed_probs(2)
-    transposed_probs(3)
+    for b in range(HALF, BLOCKS):
+        transposed_probs(b)
 
     up = remote(m["normed"].at[:, 0:32, :], m["bot"], m["srow"].at[0], m["qrow"].at[0], above)
     down = remote(m["normed"].at[:, 32:64, :], m["top"], m["srow"].at[1], m["qrow"].at[1], below)
     gup = remote(m["stop"], m["gbot"], m["srow"].at[2], m["qrow"].at[2], above)
     gdown = remote(m["sbot"], m["gtop"], m["srow"].at[3], m["qrow"].at[3], below)
+    def place(at, plane):
+        flat = plane.astype(F32).reshape(FR * COLS, CH)
+        left, right = column_shifts(flat)
+        for t, values in enumerate((left, flat, right)):
+            values = values.astype(BF).reshape(FR, COLS, CH)
+            x3[:, at, :, 256 * t : 256 * t + 256] = values[:, :, :256]
+            x3[:, at, :, 768 + 64 * t : 832 + 64 * t] = values[:, :, 256:]
+        x3[:, at, :, 960:1024] = jnp.zeros((FR, COLS, 64), BF)
+
     for b in range(BLOCKS):
         arrive(outs[b])
         x = lat_ref[:, BC * b : BC * b + BC, :].astype(F32)
@@ -417,21 +430,12 @@
         m["motion"][:, BC * b : BC * b + BC, :] = moved
         moved = moved.astype(F32)
         m["normed"][:, BC * b : BC * b + BC, :] = (moved * rms_scale(moved) * sgain).astype(BF)
-        if b == 1:
+        if b == BLOCKS // 2 - 1:
             pl.when(has_above)(lambda: up.start())
-        if b == 3:
+            place(1, m["normed"][:, 0:32, :])
+        if b == BLOCKS - 1:
             pl.when(has_below)(lambda: down.start())
 
-    def place(at, plane):
-        flat = plane.astype(F32).reshape(FR * COLS, CH)
-        left, right = column_shifts(flat)
-        for t, values in enumerate((left, flat, right)):
-            values = values.astype(BF).reshape(FR, COLS, CH)
-            x3[:, at, :, 256 * t : 256 * t + 256] = values[:, :, :256]
-            x3[:, at, :, 768 + 64 * t : 832 + 64 * t] = values[:, :, 256:]
-        x3[:, at, :, 960:1024] = jnp.zeros((FR, COLS, 64), BF)
-
-    place(1, m["normed"][:, 0:32, :])
     place(2, m["normed"][:, 32:64, :])
 
     def add_taps(dy, n):
@@ -463,11 +467,9 @@
 
     for load in loads[6:]:
         load.wait()
-    total = m["motion"][...].astype(F32).reshape(FR * CELLS, CH)
     c0, c1 = math.sqrt(2.0 / math.pi), 0.044715
     for n in range(5):
         u = m["pre"][:, 256 * n : 256 * n + 256] + add_taps(0, n) + add_taps(2, n)
-        proj = projt_ref[:, 256 * n : 256 * n + 256]
         dact = m["dact"][:, 256 * n : 256 * n + 256]
         sq = u * u
         th = jnp.tanh(c0 * u * (1.0 + c1 * sq))
@@ -475,8 +477,7 @@
         act = u * half
         slope = half + 0.5 * u * (1.0 - th * th) * (c0 + (3.0 * c0 * c1) * sq)
         dpre[:, 256 * n : 256 * n + 256] = (slope * dact).astype(BF)
-        total = total + mm_nt(act.astype(BF), proj)
-    out_ref[...] = total.astype(BF).reshape(FR, CELLS, CH)
+        m["act"][:, 256 * n : 256 * n + 256] = act.astype(BF)
 
     def back_taps(dy):
         g = [mm_nt(dpre[...], wbuf[dy, 256 * j : 256 * j + 256, :]) for j in range(4)]
@@ -515,8 +516,8 @@
         )
         m["dmot"][:, cells, :] = d
         d = (0.5 * d).astype(BF)
-        for b in (2 * r, 2 * r + 1):
-            blocks["cext"][b][8:16] = d[:, BC * (b - 2 * r) : BC * (b - 2 * r) + BC]
+        for j in range(HALF):
+            blocks["cext"][HALF * r + j][8:16] = d[:, BC * j : BC * j + BC]
 
     def send_halo(b):
         return start(*halo_copies(blocks["cext"][b], m["s3"], m["q3"], b, before, after))
@@ -527,7 +528,7 @@
         keep[:, 1] = keep[:, 1] + m["gbot"][...].astype(F32)
 
     row_cotangent(1)
-    ins = {b: send_halo(b) for b in (2, 3)}
+    ins = {b: send_halo(b) for b in range(HALF, BLOCKS)}
 
     @pl.when(has_above)
     def _():
@@ -535,32 +536,35 @@
         keep[:, 0] = keep[:, 0] + m["gtop"][...].astype(F32)
 
     row_cotangent(0)
-    ins.update({b: send_halo(b) for b in (0, 1)})
-
-    transposed_probs(0)
-    transposed_probs(1)
+    ins.update({b: send_halo(b) for b in range(HALF)})
+
+    total = mm_nt(m["act"][...], projt_ref[...]).reshape(FR, CELLS, CH)
+    out_ref[...] = (m["motion"][...].astype(F32) + total).astype(BF)
+
+    for b in range(HALF):
+        transposed_probs(b)
     outs = {}
 
     def give_back(b):
-        found = mm_nt(m["dz"][256 * b : 256 * b + 256, :], wp[...])
+        found = mm_nt(m["dz"][BR * b : BR * b + BR, :], wp[...])
         blocks["dh"][b][...] = from_groups(found).astype(BF)
         outs[b] = start(
             *return_copies(blocks["dh"][b], blocks["dback"][b], m["s4"], m["q4"], b, before, after)
         )
 
-    for b in (2, 3, 0, 1):
+    for b in (*range(HALF, BLOCKS), *range(HALF)):
         arrive(ins[b])
         for g, found in enumerate(cell_groups(blocks["cext"][b][pl.ds(shift, 16)])):
-            m["call"][256 * b + 128 * g : 256 * b + 128 * g + 128, :] = found.astype(BF)
-        dm = mm_nt(m["call"][256 * b : 256 * b + 256, :], wop[...]).astype(BF)
-        for g in (2 * b, 2 * b + 1):
+            m["call"][BR * b + 128 * g : BR * b + 128 * g + 128, :] = found.astype(BF)
+        dm = mm_nt(m["call"][BR * b : BR * b + BR, :], wop[...]).astype(BF)
+        for g in range(BG * b, BG * b + BG):
             at = slice(128 * g, 128 * g + 128)
             for i in range(HEADS // 2):
                 lanes = slice(128 * i, 128 * i + 128)
                 q = z_pair(g, i, 0)
                 kst = both_heads(z_pair(g, i, 1), first)
                 vst = both_heads(z_pair(g, i, 2), first)
-                dmi = dm[128 * (g - 2 * b) : 128 * (g - 2 * b) + 128, lanes]
+                dmi = dm[128 * (g - BG * b) : 128 * (g - BG * b) + 128, lanes]
                 pt = m["pt"][4 * g + i]
                 pf = pt.astype(F32)
                 dp = mm_nt(vst, dmi)
@@ -581,8 +585,7 @@
                 m["dz"][at, 2 * PADQ + 128 * i : 2 * PADQ + 128 * i + 128] = jnp.where(
                     first, dv[:128], dv[128:]
                 ).astype(BF)
-        if b > 1:
-            give_back(b)
+        give_back(b)
 
     flats = [m[f"flat{j}"] for j in range(3)]
     dw = mm(m["hallt"][...], m["dz"][...])
@@ -610,22 +613,20 @@
     a = [[m[f"a{k}{j}"] for j in range(3)] for k in range(4)]
     r = [[m[f"r{k}{j}"] for j in range(3)] for k in range(4)]
 
-    def gather(j, carry):
-        to = place_of(j // 2, (j % 2) * 2)
-        for c in range(2):
-            for part, order in enumerate(ORDERS):
-                index = (to[order[0]] * 4 + to[order[1]]) * 4 + to[order[2]]
-                a[0][part][c, index] = flats[part][pl.ds(25 * j + 12 * c, 16), :].astype(BF)
-        return carry
-
-    lax.fori_loop(0, 64, gather, 0)
     core = me["core"]
-    stage = [
-        start(
-            remote(a[0][p].at[1 - core], r[0][p], m["ssum"].at[p, 0], m["qsum"].at[p, 0], twin)
+    stage = []
+    for p, order in enumerate(ORDERS):
+        for j in range(64):
+            to = place_of(j // 2, (j % 2) * 2)
+            index = (to[order[0]] * 4 + to[order[1]]) * 4 + to[order[2]]
+            for c in range(2):
+                first_row = 25 * j + 12 * c
+                a[0][p][c, index] = flats[p][first_row : first_row + 16, :].astype(BF)
+        stage.append(
+            start(
+                remote(a[0][p].at[1 - core], r[0][p], m["ssum"].at[p, 0], m["qsum"].at[p, 0], twin)
+            )
         )
-        for p in range(3)
-    ]
 
     def fan_out(part, level):
         axis = ORDERS[part][level - 1]
@@ -659,19 +660,19 @@
             x, mgain, d_hidden
         )
 
-    give_back(0)
-    give_back(1)
     for p in range(3):
         arrive(stage[p])
         a[1][p][...] = (a[0][p][core].astype(F32) + r[0][p][...].astype(F32)).astype(BF)
         stage[p] = fan_out(p, 1)
-    for b in (2, 3, 0, 1):
+    for b in range(HALF, BLOCKS):
         finish(b)
     for level in (2, 3):
         for p in range(3):
             arrive(stage[p])
             a[level][p][...] = gathered(p, level - 1).astype(BF)
             stage[p] = fan_out(p, level)
+        if level - 2 < HALF:
+            finish(level - 2)
     for p in range(3):
         arrive(stage[p])
         m["sums"][p] = gathered(p, 3)[0] * (1.0 / 256.0)

time: 84.2 us -> 80.3 us (0.954)
  Pallas kernels: 81.2 us -> 77.4 us
    pallas_call x1, Pallas kernels: 79.6 us -> 75.7 us  [on_device(): pl.pallas_call(step_kernel, out_shape=(VMEM((FR, CELLS, CH), BF), VMEM((F...]
where the time goes in v2:
time: 80.3 us; the launch traced here: 80.2 us
  Pallas kernels  77.4 us (96%)
  between operations  2.12 us (3%)
    pallas_call x1, Pallas kernels, on_device(): pl.pallas_call(step_kernel, out_shape=(VMEM((FR, CELLS, CH), BF), VMEM((F...  75.7 us
    pallas_call x1, Pallas kernels, on_device(): pl.pallas_call(copy_kernel, out_shape=(shaped(FR, CELLS, CH), shaped(FR,...  1.63 us

profile of v2, /device:TPU:0, one launch (start us, length us, event | category | flops | bytes accessed | tf_op | source)
XLA Modules:
  0.0 80.2 jit_solution(2685181798944915416)
XLA Ops:
  1.9 0.1 fusion
  2.0 0.6 pad_maximum_fusion.emb_ref
  2.6 75.7 %step.1 = (bf16[8,64,320]{2,1,0:T(8,128)(2,1)S(1)}, f32[8,64,320]{2,1,0:T(8,128)S(1)}, f32[32,128]{1,0:T(8,128)S(1)}) custom-call(s32[1]{0:T(128)S(6)} %copy.14.shift_ref, bf16[8,64,320]{2,1,0:T(8,128)(2,1)} %bitcast.7, f32[320]{0:T(512)} %mgain_ref.1, f32[320]{0:T(512)} %sgain_ref.1, f32[1,320]{1,0:T(1,128)} %pad_maximum_fusion.emb_ref, f32[320,320]{1,0:T(8,128)} %tw_hbm.1, ...), custom_call_target="tpu_custom_call" | custom-call | tf_op jit(solution)/shard_map/step/pallas_call | solution.py:733
  78.4 1.6 %results.1 = (bf16[8,64,320]{2,1,0:T(8,128)(2,1)}, f32[8,64,320]{2,1,0:T(8,128)}, f32[4000]{0:T(1024)}) custom-call(bf16[8,64,320]{2,1,0:T(8,128)(2,1)S(1)} %get-tuple-element.9.out_in, f32[8,64,320]{2,1,0:T(8,128)S(1)} %get-tuple-element.10.gin_in, f32[32,128]{1,0:T(8,128)S(1)} %get-tuple-element.11.line_in), custom_call_target="tpu_custom_call" | custom-call | tf_op jit(solution)/shard_map/results/pallas_call | solution.py:748

commit v3 on v2

--- a/solution.py
+++ b/solution.py
@@ -251,6 +251,7 @@
         "act": VMEM((FR * CELLS, HID), BF),
         "dact": VMEM((FR * CELLS, HID), F32),
         "hallt": VMEM((384, 1024), BF),
+        "kt": VMEM((PADQ, 1024), BF),
         "mallt": VMEM((PADQ, 1024), BF),
         "pick": VMEM((PADQ, 384), BF),
         "tw": VMEM((CH, CH), F32),
@@ -405,6 +406,7 @@
 
     m["hallt"][...] = m["hall"][...].T
     m["mallt"][...] = m["mall"][...].T
+    m["kt"][...] = m["z"][:, PADQ : 2 * PADQ].T
     for b in range(HALF, BLOCKS):
         transposed_probs(b)
 
@@ -559,31 +561,34 @@
         dm = mm_nt(m["call"][BR * b : BR * b + BR, :], wop[...]).astype(BF)
         for g in range(BG * b, BG * b + BG):
             at = slice(128 * g, 128 * g + 128)
-            for i in range(HEADS // 2):
-                lanes = slice(128 * i, 128 * i + 128)
-                q = z_pair(g, i, 0)
-                kst = both_heads(z_pair(g, i, 1), first)
-                vst = both_heads(z_pair(g, i, 2), first)
-                dmi = dm[128 * (g - BG * b) : 128 * (g - BG * b) + 128, lanes]
-                pt = m["pt"][4 * g + i]
-                pf = pt.astype(F32)
-                dp = mm_nt(vst, dmi)
-                t = pf * dp
-                ds = jnp.concatenate(
-                    [
-                        (t[:128] - pf[:128] * jnp.sum(t[:128], axis=0, keepdims=True)) * SCALE,
-                        (t[128:] - pf[128:] * jnp.sum(t[128:], axis=0, keepdims=True)) * SCALE,
-                    ],
-                    axis=0,
+            pairs = range(HEADS // 2)
+            dmi = [
+                dm[128 * (g - BG * b) : 128 * (g - BG * b) + 128, 128 * i : 128 * i + 128]
+                for i in pairs
+            ]
+            dps = [mm_nt(both_heads(z_pair(g, i, 2), first), dmi[i]) for i in pairs]
+            dss = []
+            for i in pairs:
+                pf = m["pt"][4 * g + i].astype(F32)
+                t = pf * dps[i]
+                ds = [
+                    (t[h] - pf[h] * jnp.sum(t[h], axis=0, keepdims=True)) * SCALE
+                    for h in (slice(0, 128), slice(128, 256))
+                ]
+                dss.append(jnp.concatenate(ds, axis=0).astype(BF))
+            for i in pairs:
+                dv = mm(m["pt"][4 * g + i], dmi[i])
+                m["dz"][at, 2 * PADQ + 128 * i : 2 * PADQ + 128 * i + 128] = jnp.where(
+                    first, dv[:128], dv[128:]
                 ).astype(BF)
-                m["dz"][at, lanes] = mm_tn(ds, kst).astype(BF)
-                dk = mm(ds, q)
+            for i in pairs:
+                ds = dss[i]
+                kt = m["kt"][128 * i : 128 * i + 128, at]
+                dq = jnp.concatenate([mm(kt[:HP], ds[:128]), mm(kt[HP:], ds[128:])], axis=0)
+                m["dz"][at, 128 * i : 128 * i + 128] = dq.T.astype(BF)
+                dk = mm(ds, z_pair(g, i, 0))
                 m["dz"][at, PADQ + 128 * i : PADQ + 128 * i + 128] = jnp.where(
                     first, dk[:128], dk[128:]
-                ).astype(BF)
-                dv = mm(pt, dmi)
-                m["dz"][at, 2 * PADQ + 128 * i : 2 * PADQ + 128 * i + 128] = jnp.where(
-                    first, dv[:128], dv[128:]
                 ).astype(BF)
         give_back(b)
 

time: 80.3 us -> 77.7 us (0.968)
  Pallas kernels: 77.4 us -> 74.7 us
    pallas_call x1, Pallas kernels: 75.7 us -> 73.1 us  [on_device(): pl.pallas_call(step_kernel, out_shape=(VMEM((FR, CELLS, CH), BF), VMEM((F...]
where the time goes in v3:
time: 77.7 us; the launch traced here: 77.5 us
  Pallas kernels  74.7 us (96%)
  between operations  2.12 us (3%)
    pallas_call x1, Pallas kernels, on_device(): pl.pallas_call(step_kernel, out_shape=(VMEM((FR, CELLS, CH), BF), VMEM((F...  73.1 us
    pallas_call x1, Pallas kernels, on_device(): pl.pallas_call(copy_kernel, out_shape=(shaped(FR, CELLS, CH), shaped(FR,...  1.63 us

profile of v3, /device:TPU:0, one launch (start us, length us, event | category | flops | bytes accessed | tf_op | source)
XLA Modules:
  0.0 77.5 jit_solution(17706324734189292461)
XLA Ops:
  1.9 0.1 fusion
  2.0 0.6 pad_maximum_fusion.emb_ref
  2.6 73.1 %step.1 = (bf16[8,64,320]{2,1,0:T(8,128)(2,1)S(1)}, f32[8,64,320]{2,1,0:T(8,128)S(1)}, f32[32,128]{1,0:T(8,128)S(1)}) custom-call(s32[1]{0:T(128)S(6)} %copy.14.shift_ref, bf16[8,64,320]{2,1,0:T(8,128)(2,1)} %bitcast.7, f32[320]{0:T(512)} %mgain_ref.1, f32[320]{0:T(512)} %sgain_ref.1, f32[1,320]{1,0:T(1,128)} %pad_maximum_fusion.emb_ref, f32[320,320]{1,0:T(8,128)} %tw_hbm.1, ...), custom_call_target="tpu_custom_call" | custom-call | tf_op jit(solution)/shard_map/step/pallas_call | solution.py:738
  75.7 1.6 %results.1 = (bf16[8,64,320]{2,1,0:T(8,128)(2,1)}, f32[8,64,320]{2,1,0:T(8,128)}, f32[4000]{0:T(1024)}) custom-call(bf16[8,64,320]{2,1,0:T(8,128)(2,1)S(1)} %get-tuple-element.9.out_in, f32[8,64,320]{2,1,0:T(8,128)S(1)} %get-tuple-element.10.gin_in, f32[32,128]{1,0:T(8,128)S(1)} %get-tuple-element.11.line_in), custom_call_target="tpu_custom_call" | custom-call | tf_op jit(solution)/shard_map/results/pallas_call | solution.py:753

commit v4 on v3

--- a/solution.py
+++ b/solution.py
@@ -260,7 +260,7 @@
         "projt": VMEM((CH, HID), BF),
         "cot": VMEM((FR, CELLS, CH), BF),
         "line": VMEM((48, 128), F32),
-        "sums": VMEM((3, 16, 128), F32),
+        "sums": VMEM((3, 24, 128), F32),
         "osem": dma((5,)),
         "wsem": dma((18,)),
         **{name: dma((2, BLOCKS)) for name in ("s1", "q1", "s2", "q2", "s3", "q3", "s4", "q4")},
@@ -477,7 +477,7 @@
         th = jnp.tanh(c0 * u * (1.0 + c1 * sq))
         half = 0.5 + 0.5 * th
         act = u * half
-        slope = half + 0.5 * u * (1.0 - th * th) * (c0 + (3.0 * c0 * c1) * sq)
+        slope = half + act * (1.0 - half) * (2.0 * c0 + (6.0 * c0 * c1) * sq)
         dpre[:, 256 * n : 256 * n + 256] = (slope * dact).astype(BF)
         m["act"][:, 256 * n : 256 * n + 256] = act.astype(BF)
 
@@ -680,7 +680,7 @@
             finish(level - 2)
     for p in range(3):
         arrive(stage[p])
-        m["sums"][p] = gathered(p, 3)[0] * (1.0 / 256.0)
+        m["sums"][p, 0:16] = gathered(p, 3)[0] * (1.0 / 256.0)
     sum_ref[...] = flat_line(m["sums"], m["line"], core == 1)
     for copy in sends:
         copy.wait_send()

time: 77.7 us -> 77.6 us (level)
  no operation moved by 1% of the time
where the time goes in v4:
time: 77.6 us; the launch traced here: 77.4 us
  Pallas kernels  74.6 us (96%)
  between operations  2.12 us (3%)
    pallas_call x1, Pallas kernels, on_device(): pl.pallas_call(step_kernel, out_shape=(VMEM((FR, CELLS, CH), BF), VMEM((F...  73 us
    pallas_call x1, Pallas kernels, on_device(): pl.pallas_call(copy_kernel, out_shape=(shaped(FR, CELLS, CH), shaped(FR,...  1.63 us

profile of v4, /device:TPU:0, one launch (start us, length us, event | category | flops | bytes accessed | tf_op | source)
XLA Modules:
  0.0 77.4 jit_solution(7825639332377929975)
XLA Ops:
  1.9 0.1 fusion
  2.0 0.6 pad_maximum_fusion.emb_ref
  2.6 73.0 %step.1 = (bf16[8,64,320]{2,1,0:T(8,128)(2,1)S(1)}, f32[8,64,320]{2,1,0:T(8,128)S(1)}, f32[32,128]{1,0:T(8,128)S(1)}) custom-call(s32[1]{0:T(128)S(6)} %copy.14.shift_ref, bf16[8,64,320]{2,1,0:T(8,128)(2,1)} %bitcast.7, f32[320]{0:T(512)} %mgain_ref.1, f32[320]{0:T(512)} %sgain_ref.1, f32[1,320]{1,0:T(1,128)} %pad_maximum_fusion.emb_ref, f32[320,320]{1,0:T(8,128)} %tw_hbm.1, ...), custom_call_target="tpu_custom_call" | custom-call | tf_op jit(solution)/shard_map/step/pallas_call | solution.py:738
  75.6 1.6 %results.1 = (bf16[8,64,320]{2,1,0:T(8,128)(2,1)}, f32[8,64,320]{2,1,0:T(8,128)}, f32[4000]{0:T(1024)}) custom-call(bf16[8,64,320]{2,1,0:T(8,128)(2,1)S(1)} %get-tuple-element.9.out_in, f32[8,64,320]{2,1,0:T(8,128)S(1)} %get-tuple-element.10.gin_in, f32[32,128]{1,0:T(8,128)S(1)} %get-tuple-element.11.line_in), custom_call_target="tpu_custom_call" | custom-call | tf_op jit(solution)/shard_map/results/pallas_call | solution.py:753
